TPU v7x, 32 devices: a whole 2x2x4 slice. The times are simulated.
32 devices in a mesh: group: 2 (over x), dp: 8 (over z, y), mp: 2 (over core).
Axes of the slice: x: 2, y: 2, z: 4, core: 2. Of those that a mesh axis runs over, the one named last changes fastest.
Arguments:
- teacher_hidden: bfloat16 [1024, 8192], P('dp', ('group', 'mp')), may hold values from -6 to 6
- teacher_gain: bfloat16 [8192], P(('group', 'mp')), may hold values from 0.25 to 1.75
- teacher_head: bfloat16 [8192, 8192], P(('group', 'mp')), may hold values from -0.198873782 to 0.198873782
- student_hidden: bfloat16 [1024, 4096], P('dp'), may hold values from -6 to 6
- student_head: bfloat16 [4096, 8192], P('dp', ('group', 'mp')), may hold values from -0.28125 to 0.28125
- depth_cut: int32 [16], P('dp'), may hold values from 1 to 4
Outputs:
- kl_terms: float32 [4, 1024], P(None, 'dp')
- hidden_grad: float32 [1024, 4096], P('dp', ('group', 'mp'))
- head_grad: float32 [4096, 8192], P('dp', ('group', 'mp'))
Inputs may be any that keep to these rules, and one draw needn't show every extreme that they name: `depth_cut`: each sample's number of codebooks kept.
All inputs are finite; a program needn't handle non-finite values.
Results may differ from a plain program's by a relative error of at most 0.0053.
Values may be sent and summed in bfloat16 or wider, within the bound.
A program may use at most 192 MiB of HBM per device.

v0:
```python
import jax
import jax.numpy as jnp
from jax import lax
from jax.sharding import PartitionSpec as P

DT = 8192
C = 4
V = 2048
FRAMES = 64


epsilon = 1e-05


def shards(teacher_hidden, teacher_gain, teacher_head, student_hidden, student_head, depth_cut):
    part_count = lax.axis_size(("group", "mp"))
    device_index = lax.axis_index(("group", "mp"))
    frame_count = teacher_hidden.shape[0]
    hidden_float = teacher_hidden.astype(jnp.float32)
    squares = lax.psum(jnp.sum(hidden_float * hidden_float, axis=1), ("group", "mp"))
    row_scale = lax.rsqrt(squares / DT + epsilon)
    normed = (hidden_float * row_scale[:, None] * teacher_gain.astype(jnp.float32)[None, :]).astype(
        jnp.bfloat16
    )
    student_full = lax.all_gather(student_head, "dp", axis=0, tiled=True)
    depth_rows = jnp.repeat(depth_cut, FRAMES)
    book_range = jnp.arange(C, dtype=jnp.int32)
    alive_mask = (book_range[None, :] < depth_rows[:, None]).astype(jnp.float32)
    depth_weight = alive_mask / depth_rows[:, None].astype(jnp.float32)
    row_total = frame_count // part_count
    sliced = normed
    teacher_rows = lax.psum_scatter(
        jnp.dot(sliced, teacher_head, preferred_element_type=jnp.float32),
        ("group", "mp"),
        scatter_dimension=0,
        tiled=True,
    )
    student_part = jnp.dot(student_hidden, student_full, preferred_element_type=jnp.float32)
    student_rows = lax.all_to_all(
        student_part, ("group", "mp"), split_axis=0, concat_axis=1, tiled=True
    )
    teacher_log = jax.nn.log_softmax(teacher_rows.reshape(row_total, C, V), axis=2)
    student_log = jax.nn.log_softmax(student_rows.reshape(row_total, C, V), axis=2)
    teacher_prob = jnp.exp(teacher_log)
    divergence = jnp.sum(teacher_prob * (teacher_log - student_log), axis=2)
    weight_rows = lax.dynamic_slice_in_dim(depth_weight, device_index * row_total, row_total, 0)
    kl_terms = lax.all_gather((divergence * weight_rows).T, ("group", "mp"), axis=1, tiled=True)
    grad_rows = (
        ((jnp.exp(student_log) - teacher_prob) * weight_rows[:, :, None])
        .reshape(row_total, C * V)
        .astype(jnp.bfloat16)
    )
    score_grad = lax.all_to_all(grad_rows, ("group", "mp"), split_axis=1, concat_axis=0, tiled=True)
    hidden_term = lax.dot_general(
        score_grad, student_full, (((1,), (1,)), ((), ())), preferred_element_type=jnp.float32
    )
    head_dims = (((0,), (0,)), ((), ()))
    hidden_grad = lax.psum_scatter(hidden_term, ("group", "mp"), scatter_dimension=1, tiled=True)
    sliced = student_hidden
    head_grad = lax.psum_scatter(
        lax.dot_general(sliced, score_grad, head_dims, preferred_element_type=jnp.float32),
        "dp",
        scatter_dimension=0,
        tiled=True,
    )
    return (kl_terms, hidden_grad, head_grad)


def solution(mesh):
    return jax.shard_map(
        shards,
        mesh=mesh,
        in_specs=(
            P("dp", ("group", "mp")),
            P(("group", "mp")),
            P(("group", "mp"), None),
            P("dp", None),
            P("dp", ("group", "mp")),
            P("dp"),
        ),
        out_specs=(P(None, "dp"), P("dp", ("group", "mp")), P("dp", ("group", "mp"))),
        check_vma=False,
    )
```

profile of v0, /device:TPU:2, one launch (start us, length us, event | category | flops | bytes accessed | tf_op | source)
XLA Modules:
  0.0 875.8 jit_solution(1709255880861521296)
XLA Ops:
  8.0 0.0 copy-start
  8.0 0.0 all-gather.3.cloned.1.call-start
  8.1 0.7 all-gather.3.cloned.1.call-update
  8.7 0.0 reduce-scatter.4.cloned.1.call-start
  8.8 0.7 convert_element_type.25
  9.5 1.2 fusion.8
  10.7 5.8 psum.7
  16.5 19.5 %fusion.14 = f32[128,8192]{1,0:T(8,128)} fusion(bf16[2048,8192]{1,0:T(8,128)(2,1)} %param.9, bf16[128,2048]{1,0:T(8,128)(2,1)} %param.7, f32[2048]{0:T(1024)S(1)} %convert_element_type.25, f32[128]{0:T(128)S(1)} %add_rsqrt_fusion), kind=kOutput, calls=%fused_computation.23 | convolution fusion | flops 4296015872 | bytes 38281728 | tf_op jit(solution)/shard_map/dot_general | solution.py:33
  36.0 0.0 copy-start.2
  36.0 0.0 reduce-scatter.4.cloned.1.call-update
  36.0 203.8 %all-gather.3.cloned.1.call-done = bf16[4096,2048]{1,0:T(8,128)(2,1)} async-done(((bf16[512,2048]{1,0:T(8,128)(2,1)}), bf16[4096,2048]{1,0:T(8,128)(2,1)}) %all-gather.3.cloned.1.call-update) | async-done | bytes 16777232 | tf_op jit(solution)/shard_map/all_gather | solution.py:25
  239.8 0.0 copy-done
  239.9 9.1 %fusion.19 = f32[128,2048]{1,0:T(8,128)} fusion(bf16[128,4096]{1,0:T(8,128)(2,1)S(1)} %copy-done, bf16[4096,2048]{1,0:T(8,128)(2,1)} %all-gather.3.cloned.1.call-done), kind=kOutput, calls=%fused_computation.32 | convolution fusion | flops 2147483648 | bytes 18874368 | tf_op jit(solution)/shard_map/dot_general | solution.py:38
  249.0 4.0 all-to-all-start
  253.0 0.0 reduce-scatter.8.cloned.1.call-start
  253.0 0.0 copy-done.2
  253.0 0.1 broadcast_in_dim.2
  253.1 0.1 lt.19
  253.2 0.0 reduce-scatter.4.cloned.1.call-done
  253.2 1.9 reshape.34
  255.2 0.2 reduce_max.13
  255.4 0.1 copy.15
  255.5 10.4 %all-to-all-done = f32[4,32,2048]{2,1,0:T(8,128)S(1)} async-done(((f32[4,32,2048]{2,1,0:T(8,128)}), f32[4,32,2048]{2,1,0:T(8,128)S(1)}, u32[]{:S(2)}, u32[]{:S(2)}) %all-to-all-start) | async-done | bytes 1048608 | tf_op jit(solution)/shard_map/all_to_all | solution.py:39
  265.8 0.5 fusion.3
  266.3 0.6 fusion.7
  266.9 2.1 multiply_reduce_fusion
  269.0 0.1 multiply_bitcast_fusion
  269.1 0.3 multiply_convert_fusion
  269.5 11.2 %all_to_all.32 = bf16[32,4,2048]{2,0,1:T(8,128)(2,1)S(1)} all-to-all(bf16[32,4,2048]{2,0,1:T(8,128)(2,1)S(1)} %multiply_convert_fusion), channel_id=1, replica_groups=mesh['group'=2,'dp'=8,'mp'=2] {'group','mp'}, dimensions={1} | all-to-all | bytes 1048576 | tf_op jit(solution)/shard_map/all_to_all | solution.py:53
  280.7 13.1 %convolution_bitcast_fusion = f32[4096,2048]{0,1:T(8,128)} fusion(bf16[128,2048]{1,0:T(8,128)(2,1)S(1)} %bitcast.35, bf16[128,4096]{1,0:T(8,128)(2,1)S(1)} %copy-done), kind=kOutput, calls=%fused_computation.3 | convolution fusion | flops 2147483648 | bytes 35127296 | tf_op jit(solution)/shard_map/dot_general | solution.py:61
  293.8 0.0 reduce-scatter.8.cloned.1.call-update
  293.8 0.0 copy-start.1
  293.8 0.0 reduce-scatter.6.cloned.1.call-start
  293.9 12.8 %fusion.20 = f32[128,4096]{1,0:T(8,128)} fusion(bf16[128,2048]{1,0:T(8,128)(2,1)S(1)} %bitcast.36, bf16[4096,2048]{1,0:T(8,128)(2,1)} %all-gather.3.cloned.1.call-done), kind=kOutput, calls=%fused_computation.33 | convolution fusion | flops 2147483648 | bytes 19398656 | tf_op jit(solution)/shard_map/dot_general | solution.py:54
  306.6 0.0 reduce-scatter.6.cloned.1.call-update
  306.6 5.6 all-gather
  312.2 0.7 reshape.36
  312.9 523.0 %reduce-scatter.8.cloned.1.call-done = f32[512,2048]{0,1:T(8,128)} async-done(((f32[4096,2048]{0,1:T(8,128)}), f32[512,2048]{0,1:T(8,128)}) %reduce-scatter.8.cloned.1.call-update) | async-done | bytes 4194320 | tf_op jit(solution)/shard_map/reduce_scatter | solution.py:60
  835.9 5.3 copy.18
  841.2 27.4 %reduce-scatter.6.cloned.1.call-done = f32[128,1024]{1,0:T(8,128)} async-done(((f32[128,4096]{1,0:T(8,128)}), f32[128,1024]{1,0:T(8,128)}) %reduce-scatter.6.cloned.1.call-update) | async-done | bytes 524304 | tf_op jit(solution)/shard_map/reduce_scatter | solution.py:58
  868.6 0.0 copy-done.1
  (4 shorter events, 0.0 us)
Async XLA Ops:
  8.0 231.9 %copy-start = (bf16[128,4096]{1,0:T(8,128)(2,1)S(1)}, bf16[128,4096]{1,0:T(8,128)(2,1)}, u32[]{:S(2)}) copy-start(bf16[128,4096]{1,0:T(8,128)(2,1)} %param.10) | copy-start | bytes 3145732
  8.0 231.8 %all-gather.3.cloned.1.call-start = ((), (), s32[]{:S(2)}) async-start(), calls=%async_computation.6 | async-start | bytes 18874368 | tf_op jit(solution)/shard_map/all_gather | solution.py:25
  8.7 244.5 %reduce-scatter.4.cloned.1.call-start = ((), (), s32[]{:S(2)}) async-start(), calls=%async_computation.5 | async-start | bytes 5242880 | tf_op jit(solution)/shard_map/reduce_scatter | solution.py:32
  36.0 217.0 %copy-start.2 = (s32[2]{0:T(128)S(1)}, s32[2]{0:T(128)}, u32[]{:S(2)}) copy-start(s32[2]{0:T(128)} %param.12) | copy-start | bytes 28
  249.0 16.8 %all-to-all-start = ((f32[4,32,2048]{2,1,0:T(8,128)}), f32[4,32,2048]{2,1,0:T(8,128)S(1)}, u32[]{:S(2)}, u32[]{:S(2)}) async-start(f32[4,32,2048]{2,1,0:T(8,128)} %bitcast), calls=%async_computation.1 | async-start | bytes 2097152 | tf_op jit(solution)/shard_map/all_to_all | solution.py:39
  253.0 582.9 %reduce-scatter.8.cloned.1.call-start = ((), (), s32[]{:S(2)}) async-start(), calls=%async_computation.8 | async-start | bytes 37748736 | tf_op jit(solution)/shard_map/reduce_scatter | solution.py:60
  293.8 574.8 %copy-start.1 = (bf16[128,4096]{1,0:T(8,128)(2,1)S(1)}, bf16[128,4096]{1,0:T(8,128)(2,1)}, u32[]{:S(2)}) copy-start(bf16[128,4096]{1,0:T(8,128)(2,1)} %param.10) | copy-start | bytes 3145732
  293.8 574.8 %reduce-scatter.6.cloned.1.call-start = ((), (), s32[]{:S(2)}) async-start(), calls=%async_computation.7 | async-start | bytes 2621440 | tf_op jit(solution)/shard_map/reduce_scatter | solution.py:58
Sparse Core Ops, SparseCore 0:
  11.0 228.8 all-gather.2
  293.9 541.9 reduce-scatter.7
  839.2 29.4 reduce-scatter.5
Sparse Core Ops, SparseCore 1:
  36.1 44.7 reduce-scatter.3
where the time goes:
time: 879 us; the launch traced here: 876 us
  waiting for transfers between devices  765 us (87%)
  matrix products  54.5 us (6%)
  blocking collectives  22.6 us (3%)
  between operations  15.2 us (2%)
    reduce_scatter x1, waiting for transfers between devices, shards(): lax.psum_scatter(lax.dot_general(sliced, score_grad, head_dims, preferred...  523 us
    all_gather x1, waiting for transfers between devices, shards(): student_full = lax.all_gather(student_head, 'dp', axis=0, tiled=True)  204 us
    reduce_scatter x1, waiting for transfers between devices, shards(): lax.psum_scatter(hidden_term, ('group', 'mp'), scatter_dimension=1, tiled...  27.4 us
    dot_general x1, matrix products, shards(): jnp.dot(sliced, teacher_head, preferred_element_type=jnp.float32)  19.5 us
  transfers between devices with their start and end apart: 5, of which 4 were waited for; matrix products, arithmetic and copies ran while one was open for 6% of the time, Pallas kernels for 0%

commit v1 on v0

v1 whole, which is shorter than its diff:
```python
import jax
import jax.numpy as jnp
from jax import lax
from jax.sharding import PartitionSpec as P

C = 4
FRAMES = 64
PARTS = ("group", "mp")


epsilon = 1e-05


def book_share(values, op, share):
    every = lax.all_gather(values[:, 0], PARTS, axis=0)
    own = lax.axis_index(PARTS) // share
    block = lax.dynamic_slice_in_dim(every, own * share, share, 0)
    return op(block, axis=0)[:, None]


def shards(teacher_hidden, teacher_gain, teacher_head, student_hidden, student_head, depth_cut):
    part_count = lax.axis_size(PARTS)
    part = lax.axis_index(PARTS)
    frame_count = teacher_hidden.shape[0]
    row_parts = lax.axis_size("dp")
    columns = student_head.shape[1]
    entries = columns * part_count // C
    feature_total = teacher_hidden.shape[1] * part_count

    blocks = student_hidden.reshape(frame_count, row_parts, -1).transpose(1, 0, 2)
    hidden_columns = lax.all_to_all(blocks, "dp", split_axis=0, concat_axis=0, tiled=True)
    hidden_columns = hidden_columns.reshape(frame_count * row_parts, -1)
    student_part = jnp.dot(hidden_columns, student_head, preferred_element_type=jnp.float32)
    student_part, hidden_columns, teacher_hidden = lax.optimization_barrier(
        (student_part, hidden_columns, teacher_hidden)
    )
    student_scores = lax.psum_scatter(student_part, "dp", scatter_dimension=0, tiled=True)
    hidden_rows = lax.optimization_barrier(hidden_columns.T)

    hidden_float = teacher_hidden.astype(jnp.float32)
    squares = lax.psum(jnp.sum(hidden_float * hidden_float, axis=1), PARTS)
    row_scale = lax.rsqrt(squares / feature_total + epsilon)
    normed = (hidden_float * row_scale[:, None] * teacher_gain.astype(jnp.float32)[None, :]).astype(
        jnp.bfloat16
    )
    teacher_scores = lax.psum_scatter(
        jnp.dot(normed, teacher_head, preferred_element_type=jnp.float32),
        PARTS,
        scatter_dimension=1,
        tiled=True,
    )

    depth_rows = jnp.repeat(depth_cut, FRAMES)
    books = max(columns // entries, 1)
    share = max(entries // columns, 1)
    book_range = jnp.arange(books, dtype=jnp.int32) + part * books // share
    alive_mask = (book_range[None, :] < depth_rows[:, None]).astype(jnp.float32)
    depth_weight = alive_mask / depth_rows[:, None].astype(jnp.float32)

    def log_softmax(scores):
        top = jnp.max(scores, axis=-1, keepdims=True)
        if share > 1:
            top = book_share(top, jnp.max, share)
        shifted = scores - top
        total = jnp.sum(jnp.exp(shifted), axis=-1, keepdims=True)
        if share > 1:
            total = book_share(total, jnp.sum, share)
        return shifted - jnp.log(total)

    grads = []
    terms = []
    width = columns // books
    for book in range(books):
        span = slice(book * width, (book + 1) * width)
        weight = depth_weight[:, book : book + 1]
        teacher_log = log_softmax(teacher_scores[:, span])
        student_log = log_softmax(student_scores[:, span])
        teacher_prob = jnp.exp(teacher_log)
        divergence = jnp.sum(teacher_prob * (teacher_log - student_log), axis=-1, keepdims=True)
        grads.append(((jnp.exp(student_log) - teacher_prob) * weight).astype(jnp.bfloat16))
        terms.append((divergence * weight)[:, 0])
    score_grad = grads[0] if books == 1 else jnp.concatenate(grads, axis=1)
    every_term = lax.all_gather(jnp.stack(terms), PARTS, axis=0, tiled=True)
    kl_terms = jnp.sum(every_term.reshape(C, share, frame_count), axis=1)

    every_grad = lax.all_gather(score_grad, "dp", axis=0, tiled=True)
    hidden_part = lax.dot_general(
        every_grad, student_head, (((1,), (1,)), ((), ())), preferred_element_type=jnp.float32
    ).astype(jnp.bfloat16)
    hidden_part = hidden_part.reshape(row_parts, frame_count, -1)
    hidden_part = lax.all_to_all(hidden_part, "dp", split_axis=0, concat_axis=0, tiled=True)
    hidden_part = hidden_part.reshape(part_count, row_parts // part_count, frame_count, -1)
    hidden_part = lax.all_to_all(hidden_part, PARTS, split_axis=0, concat_axis=0, tiled=True)
    hidden_sum = jnp.sum(hidden_part.astype(jnp.float32), axis=0)
    hidden_grad = hidden_sum.transpose(1, 0, 2).reshape(frame_count, -1)
    head_grad = jnp.dot(hidden_rows, every_grad, preferred_element_type=jnp.float32)
    return (kl_terms, hidden_grad, head_grad)


def solution(mesh):
    return jax.shard_map(
        shards,
        mesh=mesh,
        in_specs=(
            P("dp", PARTS),
            P(PARTS),
            P(PARTS, None),
            P("dp", None),
            P("dp", PARTS),
            P("dp"),
        ),
        out_specs=(P(None, "dp"), P("dp", PARTS), P("dp", PARTS)),
        check_vma=False,
    )
```

time: 879 us -> 421 us (0.48)
  waiting for transfers between devices: 765 us -> 317 us
  matrix products: 54.5 us -> 35 us
  starting transfers between devices: 4.17 us -> 15.1 us
    reduce_scatter x3 -> x2, waiting for transfers between devices: 550 us -> 193 us  [the longest x1 151 us: shards(): lax.psum_scatter(student_part, 'dp', scatter_dimension=0, tiled=True)]
    all_gather x1, waiting for transfers between devices: 204 us -> 72.6 us  [shards(): every_grad = lax.all_gather(score_grad, 'dp', axis=0, tiled=True)]
    all_to_all x1 -> x3, waiting for transfers between devices: 10.4 us -> 50.8 us  [the longest x1 25.8 us: shards(): lax.all_to_all(blocks, 'dp', split_axis=0, concat_axis=0, tiled=True)]
    dot_general x4, matrix products: 54.5 us -> 35 us  [the longest x1 17.4 us: shards(): jnp.dot(normed, teacher_head, preferred_element_type=jnp.float32)]
    all_to_all x1 -> x0, blocking collectives: 11.2 us -> none  [shards(): lax.all_to_all(grad_rows, ('group', 'mp'), split_axis=1, concat_axis=0, t...]
    all_to_all x1 -> x3, starting transfers between devices: 4.04 us -> 15 us  [the longest x1 5.83 us: shards(): lax.all_to_all(blocks, 'dp', split_axis=0, concat_axis=0, tiled=True)]
  transfers between devices with their start and end apart: 5 -> 6, of which waited for: 4 -> 5; matrix products, arithmetic and copies ran while one was open for 6% -> 2% of each run, Pallas kernels for 0% -> 0%
where the time goes in v1:
time: 421 us; the launch traced here: 418 us
  waiting for transfers between devices  317 us (75%)
  matrix products  35 us (8%)
  blocking collectives  19.6 us (5%)
  starting transfers between devices  15.1 us (4%)
  between operations  13.9 us (3%)
  other arithmetic  11.1 us (3%)
  local copies, waits for them, and re-layouts  5.94 us (1%)
    reduce_scatter x1, waiting for transfers between devices, shards(): lax.psum_scatter(student_part, 'dp', scatter_dimension=0, tiled=True)  151 us
    all_gather x1, waiting for transfers between devices, shards(): every_grad = lax.all_gather(score_grad, 'dp', axis=0, tiled=True)  72.6 us
    reduce_scatter x1, waiting for transfers between devices, shards(): lax.psum_scatter(jnp.dot(normed, teacher_head, preferred_element_type=jnp...  41.5 us
    all_to_all x1, waiting for transfers between devices, shards(): lax.all_to_all(blocks, 'dp', split_axis=0, concat_axis=0, tiled=True)  25.8 us
    all_to_all x1, waiting for transfers between devices, shards(): lax.all_to_all(hidden_part, 'dp', split_axis=0, concat_axis=0, tiled=True)  25 us
    dot_general x1, matrix products, shards(): jnp.dot(normed, teacher_head, preferred_element_type=jnp.float32)  17.4 us
    all_gather x1, blocking collectives, shards(): every_term = lax.all_gather(jnp.stack(terms), PARTS, axis=0, tiled=True)  13.7 us
  transfers between devices with their start and end apart: 6, of which 5 were waited for; matrix products, arithmetic and copies ran while one was open for 2% of the time, Pallas kernels for 0%

profile of v1, /device:TPU:2, one launch (start us, length us, event | category | flops | bytes accessed | tf_op | source)
XLA Modules:
  0.0 417.6 jit_solution(7673706258841885198)
XLA Ops:
  7.2 0.0 copy-start
  7.2 0.0 copy-start.4
  7.2 2.4 copy.13
  9.6 5.8 %all-to-all-start = ((bf16[8,128,512]{1,2,0:T(8,128)(2,1)}), bf16[8,128,512]{1,2,0:T(8,128)(2,1)}, u32[]{:S(2)}, u32[]{:S(2)}) async-start(bf16[8,128,512]{1,2,0:T(8,128)(2,1)} %bitcast.1), calls=%async_computation | async-start | bytes 2097152 | tf_op jit(solution)/shard_map/all_to_all | solution.py:31
  15.4 0.0 reduce-scatter.3.cloned.1.call-start
  15.5 0.0 copy-done.4
  15.5 25.8 %all-to-all-done = bf16[8,128,512]{1,2,0:T(8,128)(2,1)} async-done(((bf16[8,128,512]{1,2,0:T(8,128)(2,1)}), bf16[8,128,512]{1,2,0:T(8,128)(2,1)}, u32[]{:S(2)}, u32[]{:S(2)}) %all-to-all-start) | async-done | bytes 1048608 | tf_op jit(solution)/shard_map/all_to_all | solution.py:31
  41.3 1.5 copy.14
  42.8 0.0 copy-start.2
  42.8 0.0 copy-done
  42.8 5.6 %fusion.9 = f32[1024,2048]{1,0:T(8,128)} fusion(bf16[1024,512]{1,0:T(8,128)(2,1)S(1)} %bitcast.23, bf16[512,2048]{1,0:T(8,128)(2,1)S(1)} %copy-done), kind=kOutput, calls=%fused_computation.19 | convolution fusion | flops 2147483648 | bytes 11534336 | tf_op jit(solution)/shard_map/dot_general | solution.py:33
  48.4 0.0 copy-done.2
  48.4 1.2 fusion
  49.6 5.9 %psum.7 = f32[128]{0:T(128)S(1)} all-reduce(f32[128]{0:T(128)S(1)} %fusion), channel_id=1, replica_groups=mesh['group'=2,'dp'=8,'mp'=2] {'group','mp'}, use_global_device_ids=true, to_apply=%region_1.0 | all-reduce | flops 128 | bytes 1024 | tf_op jit(solution)/shard_map/psum | solution.py:41
  55.5 17.4 %fusion.3 = f32[128,8192]{1,0:T(8,128)} fusion(bf16[2048,8192]{1,0:T(8,128)(2,1)} %param.8, bf16[128,2048]{1,0:T(8,128)(2,1)} %param.6, f32[2048]{0:T(1024)S(1)} %convert_element_type.59, f32[128]{0:T(128)S(1)} %add_rsqrt_fusion), kind=kOutput, calls=%fused_computation.11 | convolution fusion | flops 4296015872 | bytes 38281728 | tf_op jit(solution)/shard_map/dot_general | solution.py:47
  72.9 0.0 reduce-scatter.3.cloned.1.call-update
  72.9 0.0 copy-start.5
  72.9 0.0 reduce-scatter.5.cloned.1.call-start
  73.0 0.7 reduce-scatter.5.cloned.1.call-update
  73.7 0.0 all-gather.3.cloned.1.call-start
  73.7 0.0 copy-done.5
  73.8 0.1 broadcast_in_dim.2
  73.8 0.1 div.36
  73.9 41.5 %reduce-scatter.3.cloned.1.call-done = f32[128,2048]{1,0:T(8,128)} async-done(((f32[128,8192]{1,0:T(8,128)}), f32[128,2048]{1,0:T(8,128)}) %reduce-scatter.3.cloned.1.call-update) | async-done | bytes 1048592 | tf_op jit(solution)/shard_map/reduce_scatter | solution.py:46
  115.5 0.0 copy-start.1
  115.5 1.4 reduce_max.18
  116.9 1.5 exponential_reduce_fusion.1
  118.4 151.3 %reduce-scatter.5.cloned.1.call-done = f32[128,2048]{1,0:T(8,128)} async-done(((f32[1024,2048]{1,0:T(8,128)}), f32[128,2048]{1,0:T(8,128)}) %reduce-scatter.5.cloned.1.call-update) | async-done | bytes 1048592 | tf_op jit(solution)/shard_map/reduce_scatter | solution.py:37
  269.7 1.4 reduce_max.19
  271.1 1.5 exponential_reduce_fusion
  272.6 0.0 copy-done.1
  272.6 2.6 multiply_convert_fusion
  275.2 0.0 all-gather.3.cloned.1.call-update
  275.3 72.6 %all-gather.3.cloned.1.call-done = bf16[1024,2048]{1,0:T(8,128)(2,1)} async-done(((bf16[128,2048]{1,0:T(8,128)(2,1)}), bf16[1024,2048]{1,0:T(8,128)(2,1)}) %all-gather.3.cloned.1.call-update) | async-done | bytes 4194320 | tf_op jit(solution)/shard_map/all_gather | solution.py:86
  347.8 5.5 %convolution_convert_fusion = bf16[1024,512]{1,0:T(8,128)(2,1)} fusion(bf16[1024,2048]{1,0:T(8,128)(2,1)} %all-gather.3.cloned.1.call-done, bf16[512,2048]{1,0:T(8,128)(2,1)S(1)} %copy-done), kind=kOutput, calls=%fused_computation.1 | convolution fusion | flops 2148007936 | bytes 7340032 | tf_op jit(solution)/shard_map/dot_general | solution.py:87
  353.4 0.0 copy-start.3
  353.4 4.4 %all-to-all-start.1 = ((bf16[8,128,512]{2,1,0:T(8,128)(2,1)}), bf16[8,128,512]{2,1,0:T(8,128)(2,1)}, u32[]{:S(2)}, u32[]{:S(2)}) async-start(bf16[8,128,512]{2,1,0:T(8,128)(2,1)} %bitcast.27), calls=%async_computation.3 | async-start | bytes 2097152 | tf_op jit(solution)/shard_map/all_to_all | solution.py:91
  357.7 0.1 div.35
  357.8 25.0 %all-to-all-done.1 = bf16[8,128,512]{2,1,0:T(8,128)(2,1)} async-done(((bf16[8,128,512]{2,1,0:T(8,128)(2,1)}), bf16[8,128,512]{2,1,0:T(8,128)(2,1)}, u32[]{:S(2)}, u32[]{:S(2)}) %all-to-all-start.1) | async-done | bytes 1048608 | tf_op jit(solution)/shard_map/all_to_all | solution.py:91
  382.8 4.8 %all-to-all-start.2 = ((bf16[4,2,128,512]{3,2,1,0:T(8,128)(2,1)}), bf16[4,2,128,512]{3,2,1,0:T(8,128)(2,1)}, u32[]{:S(2)}, u32[]{:S(2)}) async-start(bf16[4,2,128,512]{3,2,1,0:T(8,128)(2,1)} %bitcast.7), calls=%async_computation.4 | async-start | bytes 2097152 | tf_op jit(solution)/shard_map/all_to_all | solution.py:93
  387.5 13.7 %all-gather = f32[4,1,128]{2,1,0:T(1,128)S(1)} all-gather(f32[1,1,128]{2,1,0:T(1,128)S(1)} %fusion.8), channel_id=1, replica_groups=mesh['group'=2,'dp'=8,'mp'=2] {'group','mp'}, dimensions={0}, use_global_device_ids=true | all-gather | bytes 2560 | tf_op jit(solution)/shard_map/all_gather | solution.py:83
  401.3 0.0 copy-done.3
  401.3 6.6 %fusion.10 = f32[512,2048]{1,0:T(8,128)} fusion(bf16[512,1024]{0,1:T(8,128)(2,1)S(1)} %bitcast.24, bf16[1024,2048]{1,0:T(8,128)(2,1)} %all-gather.3.cloned.1.call-done), kind=kOutput, calls=%fused_computation.20 | convolution fusion | flops 2147483648 | bytes 9437184 | tf_op jit(solution)/shard_map/dot_general | solution.py:96
  407.9 0.0 all-to-all-done.2
  407.9 1.4 convert_reduce_fusion
  409.3 0.2 copy.15
  409.5 1.0 copy.16
  410.5 0.6 copy.18
  (6 shorter events, 0.0 us)
Async XLA Ops:
  7.2 35.6 %copy-start = (bf16[512,2048]{1,0:T(8,128)(2,1)S(1)}, bf16[512,2048]{1,0:T(8,128)(2,1)}, u32[]{:S(2)}) copy-start(bf16[512,2048]{1,0:T(8,128)(2,1)} %param.10) | copy-start | bytes 6291460
  7.2 8.3 %copy-start.4 = (bf16[2048]{0:T(1024)(128)(2,1)S(1)}, bf16[2048]{0:T(1024)(128)(2,1)}, u32[]{:S(2)}) copy-start(bf16[2048]{0:T(1024)(128)(2,1)} %param.7) | copy-start | bytes 12292
  9.6 31.7 %all-to-all-start = ((bf16[8,128,512]{1,2,0:T(8,128)(2,1)}), bf16[8,128,512]{1,2,0:T(8,128)(2,1)}, u32[]{:S(2)}, u32[]{:S(2)}) async-start(bf16[8,128,512]{1,2,0:T(8,128)(2,1)} %bitcast.1), calls=%async_computation | async-start | bytes 2097152 | tf_op jit(solution)/shard_map/all_to_all | solution.py:31
  15.4 100.0 %reduce-scatter.3.cloned.1.call-start = ((), (), s32[]{:S(2)}) async-start(), calls=%async_computation.5 | async-start | bytes 5242880 | tf_op jit(solution)/shard_map/reduce_scatter | solution.py:46
  42.8 5.6 %copy-start.2 = (bf16[8,128,512]{2,1,0:T(8,128)(2,1)}, bf16[8,128,512]{2,1,0:T(8,128)(2,1)S(1)}, u32[]{:S(2)}) copy-start(bf16[8,128,512]{2,1,0:T(8,128)(2,1)S(1)} %copy.14) | copy-start | bytes 3145732
  72.9 0.8 copy-start.5
  72.9 196.8 %reduce-scatter.5.cloned.1.call-start = ((), (), s32[]{:S(2)}) async-start(), calls=%async_computation.6 | async-start | bytes 9437184 | tf_op jit(solution)/shard_map/reduce_scatter | solution.py:37
  73.7 274.1 %all-gather.3.cloned.1.call-start = ((), (), s32[]{:S(2)}) async-start(), calls=%async_computation.7 | async-start | bytes 4718592 | tf_op jit(solution)/shard_map/all_gather | solution.py:86
  115.5 157.2 %copy-start.1 = (f32[128,2048]{1,0:T(8,128)S(1)}, f32[128,2048]{1,0:T(8,128)}, u32[]{:S(2)}) copy-start(f32[128,2048]{1,0:T(8,128)} %reduce-scatter.3.cloned.1.call-done) | copy-start | bytes 3145732
  353.4 47.9 %copy-start.3 = (bf16[8,128,512]{2,1,0:T(8,128)(2,1)S(1)}, bf16[8,128,512]{2,1,0:T(8,128)(2,1)}, u32[]{:S(2)}) copy-start(bf16[8,128,512]{2,1,0:T(8,128)(2,1)} %copy-done.2) | copy-start | bytes 3145732
  353.4 29.4 %all-to-all-start.1 = ((bf16[8,128,512]{2,1,0:T(8,128)(2,1)}), bf16[8,128,512]{2,1,0:T(8,128)(2,1)}, u32[]{:S(2)}, u32[]{:S(2)}) async-start(bf16[8,128,512]{2,1,0:T(8,128)(2,1)} %bitcast.27), calls=%async_computation.3 | async-start | bytes 2097152 | tf_op jit(solution)/shard_map/all_to_all | solution.py:91
  382.8 25.1 %all-to-all-start.2 = ((bf16[4,2,128,512]{3,2,1,0:T(8,128)(2,1)}), bf16[4,2,128,512]{3,2,1,0:T(8,128)(2,1)}, u32[]{:S(2)}, u32[]{:S(2)}) async-start(bf16[4,2,128,512]{3,2,1,0:T(8,128)(2,1)} %bitcast.7), calls=%async_computation.4 | async-start | bytes 2097152 | tf_op jit(solution)/shard_map/all_to_all | solution.py:93
Sparse Core Ops, SparseCore 0:
  73.1 42.3 reduce-scatter.2
  119.5 150.1 reduce-scatter.4
  275.4 72.4 all-gather.2

commit v2 on v1

--- a/solution.py
+++ b/solution.py
@@ -43,12 +43,10 @@
     normed = (hidden_float * row_scale[:, None] * teacher_gain.astype(jnp.float32)[None, :]).astype(
         jnp.bfloat16
     )
-    teacher_scores = lax.psum_scatter(
-        jnp.dot(normed, teacher_head, preferred_element_type=jnp.float32),
-        PARTS,
-        scatter_dimension=1,
-        tiled=True,
-    )
+    teacher_part = jnp.dot(normed, teacher_head, preferred_element_type=jnp.float32)
+    teacher_part = teacher_part.reshape(frame_count, part_count, columns).transpose(1, 0, 2)
+    teacher_part = lax.all_to_all(teacher_part, PARTS, split_axis=0, concat_axis=0, tiled=True)
+    teacher_scores = jnp.sum(teacher_part, axis=0)
 
     depth_rows = jnp.repeat(depth_cut, FRAMES)
     books = max(columns // entries, 1)
@@ -84,16 +82,18 @@
     kl_terms = jnp.sum(every_term.reshape(C, share, frame_count), axis=1)
 
     every_grad = lax.all_gather(score_grad, "dp", axis=0, tiled=True)
+    every_grad, kl_terms = lax.optimization_barrier((every_grad, kl_terms))
     hidden_part = lax.dot_general(
         every_grad, student_head, (((1,), (1,)), ((), ())), preferred_element_type=jnp.float32
     ).astype(jnp.bfloat16)
     hidden_part = hidden_part.reshape(row_parts, frame_count, -1)
     hidden_part = lax.all_to_all(hidden_part, "dp", split_axis=0, concat_axis=0, tiled=True)
+    head_grad = jnp.dot(hidden_rows, every_grad, preferred_element_type=jnp.float32)
+    hidden_part, head_grad = lax.optimization_barrier((hidden_part, head_grad))
     hidden_part = hidden_part.reshape(part_count, row_parts // part_count, frame_count, -1)
     hidden_part = lax.all_to_all(hidden_part, PARTS, split_axis=0, concat_axis=0, tiled=True)
     hidden_sum = jnp.sum(hidden_part.astype(jnp.float32), axis=0)
     hidden_grad = hidden_sum.transpose(1, 0, 2).reshape(frame_count, -1)
-    head_grad = jnp.dot(hidden_rows, every_grad, preferred_element_type=jnp.float32)
     return (kl_terms, hidden_grad, head_grad)
 
 

time: 421 us -> 339 us (0.81)
  waiting for transfers between devices: 317 us -> 215 us
  blocking collectives: 19.6 us -> 42.4 us
    reduce_scatter x1, waiting for transfers between devices: 151 us -> 70.3 us  [shards(): lax.psum_scatter(student_part, 'dp', scatter_dimension=0, tiled=True)]
    reduce_scatter x1 -> x0, waiting for transfers between devices: 41.5 us -> none  [shards(): lax.psum_scatter(jnp.dot(normed, teacher_head, preferred_element_type=jnp...]
    all_to_all x0 -> x1, blocking collectives: none -> 31.5 us  [shards(): lax.all_to_all(blocks, 'dp', split_axis=0, concat_axis=0, tiled=True)]
    all_to_all x1, waiting for transfers between devices: 25.8 us -> 46.4 us  [shards(): lax.all_to_all(teacher_part, PARTS, split_axis=0, concat_axis=0, tiled=True)]
    all_to_all x1, waiting for transfers between devices: 0.01 us -> 12.8 us  [shards(): lax.all_to_all(hidden_part, PARTS, split_axis=0, concat_axis=0, tiled=True)]
    all_gather x1, blocking collectives: 13.7 us -> 5.03 us  [shards(): every_term = lax.all_gather(jnp.stack(terms), PARTS, axis=0, tiled=True)]
    all_to_all x1, waiting for transfers between devices: 25 us -> 18.1 us  [shards(): lax.all_to_all(hidden_part, 'dp', split_axis=0, concat_axis=0, tiled=True)]
    reduce_sum x0 -> x2, other arithmetic: none -> 5.34 us  [the longest x1 2.73 us: shards(): teacher_scores = jnp.sum(teacher_part, axis=0)]
  transfers between devices with their start and end apart: 6 -> 5, of which waited for: 5 -> 5; matrix products, arithmetic and copies ran while one was open for 2% -> 8% of each run, Pallas kernels for 0% -> 0%
where the time goes in v2:
time: 339 us; the launch traced here: 336 us
  waiting for transfers between devices  215 us (63%)
  blocking collectives  42.4 us (13%)
  matrix products  31 us (9%)
  between operations  14.1 us (4%)
  starting transfers between devices  13.8 us (4%)
  local copies, waits for them, and re-layouts  9.86 us (3%)
  other arithmetic  9.8 us (3%)
    reduce_scatter x1, waiting for transfers between devices, shards(): lax.psum_scatter(student_part, 'dp', scatter_dimension=0, tiled=True)  70.3 us
    all_gather x1, waiting for transfers between devices, shards(): every_grad = lax.all_gather(score_grad, 'dp', axis=0, tiled=True)  67.4 us
    all_to_all x1, waiting for transfers between devices, shards(): lax.all_to_all(teacher_part, PARTS, split_axis=0, concat_axis=0, tiled=True)  46.4 us
    all_to_all x1, blocking collectives, shards(): lax.all_to_all(blocks, 'dp', split_axis=0, concat_axis=0, tiled=True)  31.5 us
    all_to_all x1, waiting for transfers between devices, shards(): lax.all_to_all(hidden_part, 'dp', split_axis=0, concat_axis=0, tiled=True)  18.1 us
    dot_general x1, matrix products, shards(): jnp.dot(normed, teacher_head, preferred_element_type=jnp.float32)  13.2 us
    all_to_all x1, waiting for transfers between devices, shards(): lax.all_to_all(hidden_part, PARTS, split_axis=0, concat_axis=0, tiled=True)  12.8 us
  transfers between devices with their start and end apart: 5, of which 5 were waited for; matrix products, arithmetic and copies ran while one was open for 8% of the time, Pallas kernels for 0%

profile of v2, /device:TPU:2, one launch (start us, length us, event | category | flops | bytes accessed | tf_op | source)
XLA Modules:
  0.0 336.1 jit_solution(4176025358159080087)
XLA Ops:
  7.2 0.0 copy-start
  7.2 0.0 reduce-scatter.2.cloned.1.call-start
  7.2 1.8 copy.14
  9.0 31.5 %all_to_all.20 = bf16[8,128,512]{1,2,0:T(8,128)(2,1)} all-to-all(bf16[8,128,512]{1,2,0:T(8,128)(2,1)S(1)} %bitcast.34), channel_id=1, replica_groups=mesh['group'=2,'dp'=8,'mp'=2] {'dp'}, dimensions={0} | all-to-all | bytes 2097152 | tf_op jit(solution)/shard_map/all_to_all | solution.py:31
  40.5 1.5 copy.15
  42.0 0.0 copy-start.1
  42.0 0.0 copy-done
  42.0 5.6 %fusion.9 = f32[1024,2048]{1,0:T(8,128)} fusion(bf16[1024,512]{1,0:T(8,128)(2,1)S(1)} %bitcast.32, bf16[512,2048]{1,0:T(8,128)(2,1)S(1)} %copy-done), kind=kOutput, calls=%fused_computation.20 | convolution fusion | flops 2147483648 | bytes 11534336 | tf_op jit(solution)/shard_map/dot_general | solution.py:33
  47.6 0.0 copy-done.1
  47.6 0.0 copy-start.4
  47.6 0.0 copy-start.3
  47.6 0.0 reduce-scatter.2.cloned.1.call-update
  47.6 0.7 copy-done.4
  48.3 0.4 copy-done.3
  48.6 0.2 fusion
  48.8 5.9 %psum.7 = f32[128]{0:T(128)S(1)} all-reduce(f32[128]{0:T(128)S(1)} %fusion), channel_id=1, replica_groups=mesh['group'=2,'dp'=8,'mp'=2] {'group','mp'}, use_global_device_ids=true, to_apply=%region_4.5 | all-reduce | flops 128 | bytes 1024 | tf_op jit(solution)/shard_map/psum | solution.py:41
  54.7 13.2 %fusion.3 = f32[128,8192]{1,0:T(8,128)S(1)} fusion(bf16[2048,8192]{1,0:T(8,128)(2,1)} %param.8, bf16[128,2048]{1,0:T(8,128)(2,1)S(1)} %copy-done.3, f32[2048]{0:T(1024)S(1)} %convert_element_type.59, f32[128]{0:T(128)S(1)} %add_rsqrt_fusion), kind=kOutput, calls=%fused_computation.12 | convolution fusion | flops 4296015872 | bytes 38281728 | tf_op jit(solution)/shard_map/dot_general | solution.py:46
  67.9 2.5 copy.21
  70.4 0.0 copy-start.5
  70.4 5.3 %all-to-all-start.1 = ((f32[4,128,2048]{2,1,0:T(8,128)}), f32[4,128,2048]{2,1,0:T(8,128)}, u32[]{:S(2)}, u32[]{:S(2)}) async-start(f32[4,128,2048]{2,1,0:T(8,128)} %bitcast.31), calls=%async_computation.2 | async-start | bytes 8388608 | tf_op jit(solution)/shard_map/all_to_all | solution.py:48
  75.7 0.0 all-gather.3.cloned.1.call-start
  75.7 0.0 copy-done.5
  75.7 0.1 broadcast_in_dim.2
  75.8 0.1 div.35
  75.9 46.4 %all-to-all-done.1 = f32[4,128,2048]{2,1,0:T(8,128)} async-done(((f32[4,128,2048]{2,1,0:T(8,128)}), f32[4,128,2048]{2,1,0:T(8,128)}, u32[]{:S(2)}, u32[]{:S(2)}) %all-to-all-start.1) | async-done | bytes 4194336 | tf_op jit(solution)/shard_map/all_to_all | solution.py:48
  122.3 2.7 reduce_sum.62
  125.1 0.1 reduce_max.19
  125.2 0.3 exponential_reduce_fusion
  125.5 70.3 %reduce-scatter.2.cloned.1.call-done = f32[128,2048]{1,0:T(8,128)} async-done(((f32[1024,2048]{1,0:T(8,128)}), f32[128,2048]{1,0:T(8,128)}) %reduce-scatter.2.cloned.1.call-update) | async-done | bytes 1048592 | tf_op jit(solution)/shard_map/reduce_scatter | solution.py:37
  195.8 1.4 reduce_max.18
  197.2 1.5 exponential_reduce_fusion.1
  198.7 2.6 multiply_reduce_fusion
  201.3 0.0 all-gather.3.cloned.1.call-update
  201.3 0.1 div.36
  201.4 5.0 %all-gather = f32[4,1,128]{2,1,0:T(1,128)S(1)} all-gather(f32[1,1,128]{2,1,0:T(1,128)S(1)} %fusion.8), channel_id=1, replica_groups=mesh['group'=2,'dp'=8,'mp'=2] {'group','mp'}, dimensions={0}, use_global_device_ids=true | all-gather | bytes 2560 | tf_op jit(solution)/shard_map/all_gather | solution.py:81
  206.4 67.4 %all-gather.3.cloned.1.call-done = bf16[1024,2048]{1,0:T(8,128)(2,1)} async-done(((bf16[128,2048]{1,0:T(8,128)(2,1)}), bf16[1024,2048]{1,0:T(8,128)(2,1)}) %all-gather.3.cloned.1.call-update) | async-done | bytes 4194320 | tf_op jit(solution)/shard_map/all_gather | solution.py:84
  273.9 0.0 copy-start.2
  273.9 5.7 %convolution_convert_fusion = bf16[1024,512]{1,0:T(8,128)(2,1)} fusion(bf16[1024,2048]{1,0:T(8,128)(2,1)} %all-gather.3.cloned.1.call-done, bf16[512,2048]{1,0:T(8,128)(2,1)S(1)} %copy-done), kind=kOutput, calls=%fused_computation.2 | convolution fusion | flops 2148007936 | bytes 7340032 | tf_op jit(solution)/shard_map/dot_general | solution.py:86
  279.5 4.4 %all-to-all-start.2 = ((bf16[8,128,512]{2,1,0:T(8,128)(2,1)}), bf16[8,128,512]{2,1,0:T(8,128)(2,1)}, u32[]{:S(2)}, u32[]{:S(2)}) async-start(bf16[8,128,512]{2,1,0:T(8,128)(2,1)} %bitcast.37), calls=%async_computation.3 | async-start | bytes 2097152 | tf_op jit(solution)/shard_map/all_to_all | solution.py:90
  283.9 0.0 copy-done.2
  283.9 6.6 %fusion.10 = f32[512,2048]{1,0:T(8,128)} fusion(bf16[512,1024]{0,1:T(8,128)(2,1)S(1)} %bitcast.33, bf16[1024,2048]{1,0:T(8,128)(2,1)} %all-gather.3.cloned.1.call-done), kind=kOutput, calls=%fused_computation.21 | convolution fusion | flops 2147483648 | bytes 9437184 | tf_op jit(solution)/shard_map/dot_general | solution.py:91
  290.5 18.1 %all-to-all-done.2 = bf16[8,128,512]{2,1,0:T(8,128)(2,1)} async-done(((bf16[8,128,512]{2,1,0:T(8,128)(2,1)}), bf16[8,128,512]{2,1,0:T(8,128)(2,1)}, u32[]{:S(2)}, u32[]{:S(2)}) %all-to-all-start.2) | async-done | bytes 1048608 | tf_op jit(solution)/shard_map/all_to_all | solution.py:90
  308.6 4.0 %all-to-all-start.3 = ((bf16[4,2,128,512]{3,2,1,0:T(8,128)(2,1)}), bf16[4,2,128,512]{3,2,1,0:T(8,128)(2,1)S(1)}, u32[]{:S(2)}, u32[]{:S(2)}) async-start(bf16[4,2,128,512]{3,2,1,0:T(8,128)(2,1)} %bitcast.9), calls=%async_computation.4 | async-start | bytes 2097152 | tf_op jit(solution)/shard_map/all_to_all | solution.py:94
  312.7 12.8 %all-to-all-done.3 = bf16[4,2,128,512]{3,2,1,0:T(8,128)(2,1)S(1)} async-done(((bf16[4,2,128,512]{3,2,1,0:T(8,128)(2,1)}), bf16[4,2,128,512]{3,2,1,0:T(8,128)(2,1)S(1)}, u32[]{:S(2)}, u32[]{:S(2)}) %all-to-all-start.3) | async-done | bytes 1048608 | tf_op jit(solution)/shard_map/all_to_all | solution.py:94
  325.5 0.9 convert_reduce_fusion
  326.4 1.2 copy.17
  327.6 1.0 copy.18
  328.6 0.6 copy.23
  (6 shorter events, 0.0 us)
Async XLA Ops:
  7.2 34.8 %copy-start = (bf16[512,2048]{1,0:T(8,128)(2,1)S(1)}, bf16[512,2048]{1,0:T(8,128)(2,1)}, u32[]{:S(2)}) copy-start(bf16[512,2048]{1,0:T(8,128)(2,1)} %param.10) | copy-start | bytes 6291460
  7.2 188.6 %reduce-scatter.2.cloned.1.call-start = ((), (), s32[]{:S(2)}) async-start(), calls=%async_computation.5 | async-start | bytes 9437184 | tf_op jit(solution)/shard_map/reduce_scatter | solution.py:37
  42.0 5.6 %copy-start.1 = (bf16[8,128,512]{2,1,0:T(8,128)(2,1)}, bf16[8,128,512]{2,1,0:T(8,128)(2,1)S(1)}, u32[]{:S(2)}) copy-start(bf16[8,128,512]{2,1,0:T(8,128)(2,1)S(1)} %copy.15) | copy-start | bytes 3145732
  47.6 0.7 copy-start.4
  47.6 1.1 copy-start.3
  70.4 5.3 %copy-start.5 = (s32[2]{0:T(128)S(1)}, s32[2]{0:T(128)}, u32[]{:S(2)}) copy-start(s32[2]{0:T(128)} %param.11) | copy-start | bytes 28
  70.4 51.9 %all-to-all-start.1 = ((f32[4,128,2048]{2,1,0:T(8,128)}), f32[4,128,2048]{2,1,0:T(8,128)}, u32[]{:S(2)}, u32[]{:S(2)}) async-start(f32[4,128,2048]{2,1,0:T(8,128)} %bitcast.31), calls=%async_computation.2 | async-start | bytes 8388608 | tf_op jit(solution)/shard_map/all_to_all | solution.py:48
  75.7 198.1 %all-gather.3.cloned.1.call-start = ((), (), s32[]{:S(2)}) async-start(), calls=%async_computation.6 | async-start | bytes 4718592 | tf_op jit(solution)/shard_map/all_gather | solution.py:84
  273.9 10.1 %copy-start.2 = (bf16[8,128,512]{2,1,0:T(8,128)(2,1)S(1)}, bf16[8,128,512]{2,1,0:T(8,128)(2,1)}, u32[]{:S(2)}) copy-start(bf16[8,128,512]{2,1,0:T(8,128)(2,1)} %copy-done.1) | copy-start | bytes 3145732
  279.5 29.1 %all-to-all-start.2 = ((bf16[8,128,512]{2,1,0:T(8,128)(2,1)}), bf16[8,128,512]{2,1,0:T(8,128)(2,1)}, u32[]{:S(2)}, u32[]{:S(2)}) async-start(bf16[8,128,512]{2,1,0:T(8,128)(2,1)} %bitcast.37), calls=%async_computation.3 | async-start | bytes 2097152 | tf_op jit(solution)/shard_map/all_to_all | solution.py:90
  308.6 16.8 %all-to-all-start.3 = ((bf16[4,2,128,512]{3,2,1,0:T(8,128)(2,1)}), bf16[4,2,128,512]{3,2,1,0:T(8,128)(2,1)S(1)}, u32[]{:S(2)}, u32[]{:S(2)}) async-start(bf16[4,2,128,512]{3,2,1,0:T(8,128)(2,1)} %bitcast.9), calls=%async_computation.4 | async-start | bytes 2097152 | tf_op jit(solution)/shard_map/all_to_all | solution.py:94
Sparse Core Ops, SparseCore 0:
  47.7 148.0 reduce-scatter.1
  201.4 72.3 all-gather.2

commit v3 on v2

--- a/solution.py
+++ b/solution.py
@@ -35,7 +35,11 @@
         (student_part, hidden_columns, teacher_hidden)
     )
     student_scores = lax.psum_scatter(student_part, "dp", scatter_dimension=0, tiled=True)
-    hidden_rows = lax.optimization_barrier(hidden_columns.T)
+    half = frame_count // 2
+    halves = hidden_columns.reshape(row_parts, 2, half, -1)
+    hidden_rows = lax.optimization_barrier(
+        [halves[:, k].reshape(half * row_parts, -1).T for k in range(2)]
+    )
 
     hidden_float = teacher_hidden.astype(jnp.float32)
     squares = lax.psum(jnp.sum(hidden_float * hidden_float, axis=1), PARTS)
@@ -81,19 +85,30 @@
     every_term = lax.all_gather(jnp.stack(terms), PARTS, axis=0, tiled=True)
     kl_terms = jnp.sum(every_term.reshape(C, share, frame_count), axis=1)
 
-    every_grad = lax.all_gather(score_grad, "dp", axis=0, tiled=True)
-    every_grad, kl_terms = lax.optimization_barrier((every_grad, kl_terms))
-    hidden_part = lax.dot_general(
-        every_grad, student_head, (((1,), (1,)), ((), ())), preferred_element_type=jnp.float32
-    ).astype(jnp.bfloat16)
-    hidden_part = hidden_part.reshape(row_parts, frame_count, -1)
-    hidden_part = lax.all_to_all(hidden_part, "dp", split_axis=0, concat_axis=0, tiled=True)
-    head_grad = jnp.dot(hidden_rows, every_grad, preferred_element_type=jnp.float32)
-    hidden_part, head_grad = lax.optimization_barrier((hidden_part, head_grad))
-    hidden_part = hidden_part.reshape(part_count, row_parts // part_count, frame_count, -1)
-    hidden_part = lax.all_to_all(hidden_part, PARTS, split_axis=0, concat_axis=0, tiled=True)
-    hidden_sum = jnp.sum(hidden_part.astype(jnp.float32), axis=0)
-    hidden_grad = hidden_sum.transpose(1, 0, 2).reshape(frame_count, -1)
+    first = lax.all_gather(score_grad[:half], "dp", axis=0, tiled=True)
+    second = lax.all_gather(score_grad[half:], "dp", axis=0, tiled=True)
+
+    def hidden_blocks(every_grad):
+        block = lax.dot_general(
+            every_grad, student_head, (((1,), (1,)), ((), ())), preferred_element_type=jnp.float32
+        ).astype(jnp.bfloat16)
+        block = block.reshape(row_parts, half, -1)
+        return lax.all_to_all(block, "dp", split_axis=0, concat_axis=0, tiled=True)
+
+    def hidden_sum(block):
+        block = block.reshape(part_count, row_parts // part_count, half, -1)
+        block = lax.all_to_all(block, PARTS, split_axis=0, concat_axis=0, tiled=True)
+        total = jnp.sum(block.astype(jnp.float32), axis=0)
+        return total.transpose(1, 0, 2).reshape(half, -1)
+
+    first_hidden = hidden_sum(hidden_blocks(first))
+    first_hidden, second, kl_terms = lax.optimization_barrier((first_hidden, second, kl_terms))
+    second_blocks = hidden_blocks(second)
+    head_grad = jnp.dot(hidden_rows[0], first, preferred_element_type=jnp.float32) + jnp.dot(
+        hidden_rows[1], second, preferred_element_type=jnp.float32
+    )
+    second_blocks, head_grad = lax.optimization_barrier((second_blocks, head_grad))
+    hidden_grad = jnp.concatenate([first_hidden, hidden_sum(second_blocks)], axis=0)
     return (kl_terms, hidden_grad, head_grad)
 
 

time: 339 us -> 350 us (1.032)
  blocking collectives: 42.4 us -> 71.3 us
  waiting for transfers between devices: 215 us -> 195 us
  starting transfers between devices: 13.8 us -> 17.7 us
    all_to_all x0 -> x1, blocking collectives: none -> 25.9 us  [hidden_blocks(): return lax.all_to_all(block, 'dp', split_axis=0, concat_axis=0, tiled=True)]
    all_to_all x2 -> x3, waiting for transfers between devices: 30.9 us -> 14.2 us  [the longest x2 7.18 us: hidden_sum(): lax.all_to_all(block, PARTS, split_axis=0, concat_axis=0, tiled=True)]
    all_gather x1 -> x2, waiting for transfers between devices: 67.4 us -> 63 us  [the longest x1 47.7 us: shards(): first = lax.all_gather(score_grad[:half], 'dp', axis=0, tiled=True)]
    all_to_all x2 -> x3, starting transfers between devices: 8.46 us -> 12.3 us  [the longest x2 7.99 us: hidden_sum(): lax.all_to_all(block, PARTS, split_axis=0, concat_axis=0, tiled=True)]
    dot_general x2 -> x4, matrix products: 12.2 us -> 11.3 us  [the longest x2 6.62 us: hidden_blocks(): lax.dot_general(every_grad, student_head, (((1,), (1,)), ((), ())), prefe...]
  transfers between devices with their start and end apart: 5 -> 7, of which waited for: 5 -> 6; matrix products, arithmetic and copies ran while one was open for 8% -> 8% of each run, Pallas kernels for 0% -> 0%
where the time goes in v3:
time: 350 us; the launch traced here: 347 us
  waiting for transfers between devices  195 us (56%)
  blocking collectives  71.3 us (20%)
  matrix products  30 us (9%)
  starting transfers between devices  17.7 us (5%)
  between operations  13.9 us (4%)
  local copies, waits for them, and re-layouts  10.4 us (3%)
  other arithmetic  9.08 us (3%)
    reduce_scatter x1, waiting for transfers between devices, shards(): lax.psum_scatter(student_part, 'dp', scatter_dimension=0, tiled=True)  70.3 us
    all_gather x1, waiting for transfers between devices, shards(): first = lax.all_gather(score_grad[:half], 'dp', axis=0, tiled=True)  47.7 us
    all_to_all x1, waiting for transfers between devices, shards(): lax.all_to_all(teacher_part, PARTS, split_axis=0, concat_axis=0, tiled=True)  46.4 us
    all_to_all x1, blocking collectives, shards(): lax.all_to_all(blocks, 'dp', split_axis=0, concat_axis=0, tiled=True)  31.5 us
    all_to_all x1, blocking collectives, hidden_blocks(): return lax.all_to_all(block, 'dp', split_axis=0, concat_axis=0, tiled=True)  25.9 us
    all_gather x1, waiting for transfers between devices, shards(): second = lax.all_gather(score_grad[half:], 'dp', axis=0, tiled=True)  15.3 us
    dot_general x1, matrix products, shards(): jnp.dot(normed, teacher_head, preferred_element_type=jnp.float32)  13.2 us
    all_to_all x2, starting transfers between devices, hidden_sum(): lax.all_to_all(block, PARTS, split_axis=0, concat_axis=0, tiled=True)  7.99 us
  transfers between devices with their start and end apart: 7, of which 6 were waited for; matrix products, arithmetic and copies ran while one was open for 8% of the time, Pallas kernels for 0%

profile of v3, /device:TPU:2, one launch (start us, length us, event | category | flops | bytes accessed | tf_op | source)
XLA Modules:
  0.0 346.9 jit_solution(14851610409636730647)
XLA Ops:
  7.2 0.0 reduce-scatter.2.cloned.1.call-start
  7.2 1.8 copy.14
  9.0 31.5 %all_to_all.30 = bf16[8,128,512]{1,2,0:T(8,128)(2,1)} all-to-all(bf16[8,128,512]{1,2,0:T(8,128)(2,1)S(1)} %bitcast.50), channel_id=1, replica_groups=mesh['group'=2,'dp'=8,'mp'=2] {'dp'}, dimensions={0} | all-to-all | bytes 2097152 | tf_op jit(solution)/shard_map/all_to_all | solution.py:31
  40.5 1.5 copy.15
  42.0 5.6 %fusion.11 = f32[1024,2048]{1,0:T(8,128)} fusion(bf16[1024,512]{1,0:T(8,128)(2,1)S(1)} %bitcast.48, bf16[512,2048]{1,0:T(8,128)(2,1)S(1)} %copy-done), kind=kOutput, calls=%fused_computation.26 | convolution fusion | flops 2147483648 | bytes 11534336 | tf_op jit(solution)/shard_map/dot_general | solution.py:33
  47.6 0.0 reduce-scatter.2.cloned.1.call-update
  47.6 0.7 copy-done.6
  48.3 0.4 copy-done.3
  48.6 0.2 fusion
  48.8 5.9 %psum.7 = f32[128]{0:T(128)S(1)} all-reduce(f32[128]{0:T(128)S(1)} %fusion), channel_id=1, replica_groups=mesh['group'=2,'dp'=8,'mp'=2] {'group','mp'}, use_global_device_ids=true, to_apply=%region_4.5 | all-reduce | flops 128 | bytes 1024 | tf_op jit(solution)/shard_map/psum | solution.py:45
  54.7 13.2 %fusion.3 = f32[128,8192]{1,0:T(8,128)S(1)} fusion(bf16[2048,8192]{1,0:T(8,128)(2,1)} %param.8, bf16[128,2048]{1,0:T(8,128)(2,1)S(1)} %copy-done.3, f32[2048]{0:T(1024)S(1)} %convert_element_type.65, f32[128]{0:T(128)S(1)} %add_rsqrt_fusion), kind=kOutput, calls=%fused_computation.15 | convolution fusion | flops 4296015872 | bytes 38281728 | tf_op jit(solution)/shard_map/dot_general | solution.py:50
  67.9 2.5 copy.23
  70.4 5.3 %all-to-all-start.1 = ((f32[4,128,2048]{2,1,0:T(8,128)}), f32[4,128,2048]{2,1,0:T(8,128)}, u32[]{:S(2)}, u32[]{:S(2)}) async-start(f32[4,128,2048]{2,1,0:T(8,128)} %bitcast.47), calls=%async_computation.2 | async-start | bytes 8388608 | tf_op jit(solution)/shard_map/all_to_all | solution.py:52
  75.7 0.1 broadcast_in_dim.2
  75.8 0.1 div.35
  75.9 46.4 %all-to-all-done.1 = f32[4,128,2048]{2,1,0:T(8,128)} async-done(((f32[4,128,2048]{2,1,0:T(8,128)}), f32[4,128,2048]{2,1,0:T(8,128)}, u32[]{:S(2)}, u32[]{:S(2)}) %all-to-all-start.1) | async-done | bytes 4194336 | tf_op jit(solution)/shard_map/all_to_all | solution.py:52
  122.3 2.7 reduce_sum.71
  125.1 0.1 reduce_max.19
  125.2 0.3 exponential_reduce_fusion
  125.5 70.3 %reduce-scatter.2.cloned.1.call-done = f32[128,2048]{1,0:T(8,128)} async-done(((f32[1024,2048]{1,0:T(8,128)}), f32[128,2048]{1,0:T(8,128)}) %reduce-scatter.2.cloned.1.call-update) | async-done | bytes 1048592 | tf_op jit(solution)/shard_map/reduce_scatter | solution.py:37
  195.8 1.4 reduce_max.18
  197.2 1.5 exponential_reduce_fusion.1
  198.7 1.9 multiply_reduce_fusion
  200.5 0.8 fusion.10
  201.4 0.0 all-gather.4.cloned.1.call-update
  201.4 0.0 all-gather.6.cloned.1.call-start
  201.5 0.7 all-gather.6.cloned.1.call-update
  202.1 47.7 %all-gather.4.cloned.1.call-done = bf16[512,2048]{1,0:T(8,128)(2,1)} async-done(((bf16[64,2048]{1,0:T(8,128)(2,1)}), bf16[512,2048]{1,0:T(8,128)(2,1)}) %all-gather.4.cloned.1.call-update) | async-done | bytes 2097168 | tf_op jit(solution)/shard_map/all_gather | solution.py:88
  249.8 2.9 convolution_convert_fusion.1
  252.7 25.9 %all_to_all.31 = bf16[8,64,512]{2,1,0:T(8,128)(2,1)} all-to-all(bf16[8,64,512]{2,1,0:T(8,128)(2,1)S(1)} %bitcast.58), channel_id=1, replica_groups=mesh['group'=2,'dp'=8,'mp'=2] {'dp'}, dimensions={0} | all-to-all | bytes 1048576 | tf_op jit(solution)/shard_map/all_to_all | solution.py:96
  278.6 4.0 %all-to-all-start.3 = ((bf16[4,2,64,512]{3,2,1,0:T(8,128)(2,1)}), bf16[4,2,64,512]{3,2,1,0:T(8,128)(2,1)S(1)}, u32[]{:S(2)}, u32[]{:S(2)}) async-start(bf16[4,2,64,512]{3,2,1,0:T(8,128)(2,1)} %bitcast.5), calls=%async_computation.4 | async-start | bytes 1048576 | tf_op jit(solution)/shard_map/all_to_all | solution.py:100
  282.6 0.1 div.36
  282.7 8.0 %all-gather = f32[4,1,128]{2,1,0:T(1,128)S(1)} all-gather(f32[1,1,128]{2,1,0:T(1,128)S(1)} %fusion.8), channel_id=1, replica_groups=mesh['group'=2,'dp'=8,'mp'=2] {'group','mp'}, dimensions={0}, use_global_device_ids=true | all-gather | bytes 2560 | tf_op jit(solution)/shard_map/all_gather | solution.py:85
  290.7 0.1 convert_reduce_fusion.1
  290.8 15.3 %all-gather.6.cloned.1.call-done = bf16[512,2048]{1,0:T(8,128)(2,1)} async-done(((bf16[64,2048]{1,0:T(8,128)(2,1)}), bf16[512,2048]{1,0:T(8,128)(2,1)}) %all-gather.6.cloned.1.call-update) | async-done | bytes 2097168 | tf_op jit(solution)/shard_map/all_gather | solution.py:89
  306.1 3.8 %convolution_convert_fusion = bf16[512,512]{1,0:T(8,128)(2,1)} fusion(bf16[512,2048]{1,0:T(8,128)(2,1)} %all-gather.6.cloned.1.call-done, bf16[512,2048]{1,0:T(8,128)(2,1)S(1)} %copy-done), kind=kOutput, calls=%fused_computation.4 | convolution fusion | flops 1074003968 | bytes 4718592 | tf_op jit(solution)/shard_map/dot_general | solution.py:92
  309.9 4.3 %all-to-all-start.4 = ((bf16[8,64,512]{2,1,0:T(8,128)(2,1)}), bf16[8,64,512]{2,1,0:T(8,128)(2,1)}, u32[]{:S(2)}, u32[]{:S(2)}) async-start(bf16[8,64,512]{2,1,0:T(8,128)(2,1)} %bitcast.57), calls=%async_computation.5 | async-start | bytes 1048576 | tf_op jit(solution)/shard_map/all_to_all | solution.py:96
  314.2 0.1 fusion.9
  314.3 1.5 copy-done.4
  315.8 1.3 fusion.12
  317.1 0.3 copy-done.5
  317.4 3.4 convolution_add_fusion
  320.7 7.0 %all-to-all-done.4 = bf16[8,64,512]{2,1,0:T(8,128)(2,1)} async-done(((bf16[8,64,512]{2,1,0:T(8,128)(2,1)}), bf16[8,64,512]{2,1,0:T(8,128)(2,1)}, u32[]{:S(2)}, u32[]{:S(2)}) %all-to-all-start.4) | async-done | bytes 524320 | tf_op jit(solution)/shard_map/all_to_all | solution.py:96
  327.7 4.0 %all-to-all-start.5 = ((bf16[4,2,64,512]{3,2,1,0:T(8,128)(2,1)}), bf16[4,2,64,512]{3,2,1,0:T(8,128)(2,1)S(1)}, u32[]{:S(2)}, u32[]{:S(2)}) async-start(bf16[4,2,64,512]{3,2,1,0:T(8,128)(2,1)} %bitcast.16), calls=%async_computation.6 | async-start | bytes 1048576 | tf_op jit(solution)/shard_map/all_to_all | solution.py:100
  331.7 7.2 %all-to-all-done.5 = bf16[4,2,64,512]{3,2,1,0:T(8,128)(2,1)S(1)} async-done(((bf16[4,2,64,512]{3,2,1,0:T(8,128)(2,1)}), bf16[4,2,64,512]{3,2,1,0:T(8,128)(2,1)S(1)}, u32[]{:S(2)}, u32[]{:S(2)}) %all-to-all-start.5) | async-done | bytes 524320 | tf_op jit(solution)/shard_map/all_to_all | solution.py:100
  338.9 0.1 convert_reduce_fusion
  339.0 0.8 pad_maximum_fusion
  339.8 0.6 copy.25
  (22 shorter events, 0.1 us)
Async XLA Ops:
  7.2 34.8 %copy-start = (bf16[512,2048]{1,0:T(8,128)(2,1)S(1)}, bf16[512,2048]{1,0:T(8,128)(2,1)}, u32[]{:S(2)}) copy-start(bf16[512,2048]{1,0:T(8,128)(2,1)} %param.10) | copy-start | bytes 6291460
  7.2 188.6 %reduce-scatter.2.cloned.1.call-start = ((), (), s32[]{:S(2)}) async-start(), calls=%async_computation.7 | async-start | bytes 9437184 | tf_op jit(solution)/shard_map/reduce_scatter | solution.py:37
  42.0 5.6 %copy-start.1 = (bf16[8,128,512]{2,1,0:T(8,128)(2,1)}, bf16[8,128,512]{2,1,0:T(8,128)(2,1)S(1)}, u32[]{:S(2)}) copy-start(bf16[8,128,512]{2,1,0:T(8,128)(2,1)S(1)} %copy.15) | copy-start | bytes 3145732
  47.6 0.7 copy-start.6
  47.6 1.1 copy-start.3
  70.4 5.3 %copy-start.7 = (s32[2]{0:T(128)S(1)}, s32[2]{0:T(128)}, u32[]{:S(2)}) copy-start(s32[2]{0:T(128)} %param.11) | copy-start | bytes 28
  70.4 51.9 %all-to-all-start.1 = ((f32[4,128,2048]{2,1,0:T(8,128)}), f32[4,128,2048]{2,1,0:T(8,128)}, u32[]{:S(2)}, u32[]{:S(2)}) async-start(f32[4,128,2048]{2,1,0:T(8,128)} %bitcast.47), calls=%async_computation.2 | async-start | bytes 8388608 | tf_op jit(solution)/shard_map/all_to_all | solution.py:52
  75.7 174.1 %all-gather.4.cloned.1.call-start = ((), (), s32[]{:S(2)}) async-start(), calls=%async_computation.8 | async-start | bytes 2359296 | tf_op jit(solution)/shard_map/all_gather | solution.py:88
  201.4 104.7 %all-gather.6.cloned.1.call-start = ((), (), s32[]{:S(2)}) async-start(), calls=%async_computation.9 | async-start | bytes 2359296 | tf_op jit(solution)/shard_map/all_gather | solution.py:89
  278.6 12.1 %all-to-all-start.3 = ((bf16[4,2,64,512]{3,2,1,0:T(8,128)(2,1)}), bf16[4,2,64,512]{3,2,1,0:T(8,128)(2,1)S(1)}, u32[]{:S(2)}, u32[]{:S(2)}) async-start(bf16[4,2,64,512]{3,2,1,0:T(8,128)(2,1)} %bitcast.5), calls=%async_computation.4 | async-start | bytes 1048576 | tf_op jit(solution)/shard_map/all_to_all | solution.py:100
  306.1 8.1 %copy-start.2 = (bf16[8,128,512]{2,1,0:T(8,128)(2,1)S(1)}, bf16[8,128,512]{2,1,0:T(8,128)(2,1)}, u32[]{:S(2)}) copy-start(bf16[8,128,512]{2,1,0:T(8,128)(2,1)} %copy-done.1) | copy-start | bytes 3145732
  309.9 17.9 %all-to-all-start.4 = ((bf16[8,64,512]{2,1,0:T(8,128)(2,1)}), bf16[8,64,512]{2,1,0:T(8,128)(2,1)}, u32[]{:S(2)}, u32[]{:S(2)}) async-start(bf16[8,64,512]{2,1,0:T(8,128)(2,1)} %bitcast.57), calls=%async_computation.5 | async-start | bytes 1048576 | tf_op jit(solution)/shard_map/all_to_all | solution.py:96
  314.2 1.6 copy-start.4
  315.8 1.6 copy-start.5
  327.7 11.2 %all-to-all-start.5 = ((bf16[4,2,64,512]{3,2,1,0:T(8,128)(2,1)}), bf16[4,2,64,512]{3,2,1,0:T(8,128)(2,1)S(1)}, u32[]{:S(2)}, u32[]{:S(2)}) async-start(bf16[4,2,64,512]{3,2,1,0:T(8,128)(2,1)} %bitcast.16), calls=%async_computation.6 | async-start | bytes 1048576 | tf_op jit(solution)/shard_map/all_to_all | solution.py:100
Sparse Core Ops, SparseCore 0:
  47.7 148.0 reduce-scatter.1
  201.5 48.2 all-gather.3
  252.8 53.2 all-gather.5

commit v4 on v2

--- a/solution.py
+++ b/solution.py
@@ -86,14 +86,39 @@
     hidden_part = lax.dot_general(
         every_grad, student_head, (((1,), (1,)), ((), ())), preferred_element_type=jnp.float32
     ).astype(jnp.bfloat16)
-    hidden_part = hidden_part.reshape(row_parts, frame_count, -1)
-    hidden_part = lax.all_to_all(hidden_part, "dp", split_axis=0, concat_axis=0, tiled=True)
+    rounds = row_parts // part_count
+    hidden_part = hidden_part.reshape(part_count, rounds * frame_count, -1)
+    hidden_part = lax.all_to_all(hidden_part, PARTS, split_axis=0, concat_axis=0, tiled=True)
     head_grad = jnp.dot(hidden_rows, every_grad, preferred_element_type=jnp.float32)
     hidden_part, head_grad = lax.optimization_barrier((hidden_part, head_grad))
-    hidden_part = hidden_part.reshape(part_count, row_parts // part_count, frame_count, -1)
-    hidden_part = lax.all_to_all(hidden_part, PARTS, split_axis=0, concat_axis=0, tiled=True)
-    hidden_sum = jnp.sum(hidden_part.astype(jnp.float32), axis=0)
-    hidden_grad = hidden_sum.transpose(1, 0, 2).reshape(frame_count, -1)
+    hidden_sum = jnp.sum(hidden_part.astype(jnp.float32), axis=0).astype(jnp.bfloat16)
+    hidden_sum = hidden_sum.reshape(rounds, frame_count, -1)
+    row = lax.axis_index("dp")
+    cores = lax.axis_size("mp")
+
+    def spot(row_place, piece):
+        return (piece // cores * row_parts + row_place) * cores + piece % cores
+
+    arrived = []
+    for turn in range(rounds):
+        pairs = [
+            (
+                spot(source, piece),
+                spot(rounds * piece + (turn + source) % rounds, source // rounds),
+            )
+            for source in range(row_parts)
+            for piece in range(part_count)
+        ]
+        block = lax.dynamic_index_in_dim(hidden_sum, (turn + row) % rounds, 0, keepdims=False)
+        arrived.append(lax.ppermute(block, ("group", "dp", "mp"), pairs))
+    ordered = arrived
+    if rounds > 1:
+        stacked = jnp.stack(arrived)
+        ordered = [
+            lax.dynamic_index_in_dim(stacked, (row - slot + rounds) % rounds, 0, keepdims=False)
+            for slot in range(rounds)
+        ]
+    hidden_grad = jnp.concatenate(ordered, axis=1).astype(jnp.float32)
     return (kl_terms, hidden_grad, head_grad)
 
 

time: 339 us -> 323 us (0.953)
  waiting for transfers between devices: 215 us -> 200 us
    all_to_all x1 -> x0, waiting for transfers between devices: 18.1 us -> none  [shards(): lax.all_to_all(hidden_part, 'dp', split_axis=0, concat_axis=0, tiled=True)]
    ppermute x0 -> x2, waiting for transfers between devices: none -> 9.64 us  [shards(): arrived.append(lax.ppermute(block, ('group', 'dp', 'mp'), pairs))]
    all_to_all x1, waiting for transfers between devices: 12.8 us -> 6.33 us  [shards(): lax.all_to_all(hidden_part, PARTS, split_axis=0, concat_axis=0, tiled=True)]
    ppermute x0 -> x2, starting transfers between devices: none -> 5.77 us  [shards(): arrived.append(lax.ppermute(block, ('group', 'dp', 'mp'), pairs))]
    all_to_all x1 -> x0, starting transfers between devices: 4.42 us -> none  [shards(): lax.all_to_all(hidden_part, 'dp', split_axis=0, concat_axis=0, tiled=True)]
  transfers between devices with their start and end apart: 5 -> 6, of which waited for: 5 -> 6; matrix products, arithmetic and copies ran while one was open for 8% -> 8% of each run, Pallas kernels for 0% -> 0%
where the time goes in v4:
time: 323 us; the launch traced here: 322 us
  waiting for transfers between devices  200 us (62%)
  blocking collectives  42.4 us (13%)
  matrix products  31 us (10%)
  starting transfers between devices  15.9 us (5%)
  between operations  14.1 us (4%)
  other arithmetic  11.3 us (3%)
  local copies, waits for them, and re-layouts  7.65 us (2%)
    reduce_scatter x1, waiting for transfers between devices, shards(): lax.psum_scatter(student_part, 'dp', scatter_dimension=0, tiled=True)  70.3 us
    all_gather x1, waiting for transfers between devices, shards(): every_grad = lax.all_gather(score_grad, 'dp', axis=0, tiled=True)  67.4 us
    all_to_all x1, waiting for transfers between devices, shards(): lax.all_to_all(teacher_part, PARTS, split_axis=0, concat_axis=0, tiled=True)  46.4 us
    all_to_all x1, blocking collectives, shards(): lax.all_to_all(blocks, 'dp', split_axis=0, concat_axis=0, tiled=True)  31.5 us
    dot_general x1, matrix products, shards(): jnp.dot(normed, teacher_head, preferred_element_type=jnp.float32)  13.2 us
    ppermute x2, waiting for transfers between devices, shards(): arrived.append(lax.ppermute(block, ('group', 'dp', 'mp'), pairs))  9.64 us
    dot_general x1, matrix products, shards(): jnp.dot(hidden_rows, every_grad, preferred_element_type=jnp.float32)  6.57 us
  transfers between devices with their start and end apart: 6, of which 6 were waited for; matrix products, arithmetic and copies ran while one was open for 8% of the time, Pallas kernels for 0%

profile of v4, /device:TPU:2, one launch (start us, length us, event | category | flops | bytes accessed | tf_op | source)
XLA Modules:
  0.0 322.5 jit_solution(11722732979396980467)
XLA Ops:
  7.2 0.0 copy-start
  7.2 0.0 reduce-scatter.2.cloned.1.call-start
  7.2 1.8 copy.11
  9.0 31.5 %all_to_all.15 = bf16[8,128,512]{1,2,0:T(8,128)(2,1)} all-to-all(bf16[8,128,512]{1,2,0:T(8,128)(2,1)S(1)} %bitcast.42), channel_id=1, replica_groups=mesh['group'=2,'dp'=8,'mp'=2] {'dp'}, dimensions={0} | all-to-all | bytes 2097152 | tf_op jit(solution)/shard_map/all_to_all | solution.py:31
  40.5 1.5 copy.12
  42.0 0.0 copy-start.1
  42.0 0.0 copy-done
  42.0 5.6 %fusion.13 = f32[1024,2048]{1,0:T(8,128)} fusion(bf16[1024,512]{1,0:T(8,128)(2,1)S(1)} %bitcast.40, bf16[512,2048]{1,0:T(8,128)(2,1)S(1)} %copy-done), kind=kOutput, calls=%fused_computation.30 | convolution fusion | flops 2147483648 | bytes 11534336 | tf_op jit(solution)/shard_map/dot_general | solution.py:33
  47.6 0.0 copy-done.1
  47.6 0.0 copy-start.4
  47.6 0.0 copy-start.3
  47.6 0.0 reduce-scatter.2.cloned.1.call-update
  47.6 0.7 copy-done.4
  48.3 0.4 copy-done.3
  48.6 0.2 fusion
  48.8 5.9 %psum.7 = f32[128]{0:T(128)S(1)} all-reduce(f32[128]{0:T(128)S(1)} %fusion), channel_id=1, replica_groups=mesh['group'=2,'dp'=8,'mp'=2] {'group','mp'}, use_global_device_ids=true, to_apply=%region_4.5 | all-reduce | flops 128 | bytes 1024 | tf_op jit(solution)/shard_map/psum | solution.py:41
  54.7 13.2 %fusion.3 = f32[128,8192]{1,0:T(8,128)S(1)} fusion(bf16[2048,8192]{1,0:T(8,128)(2,1)} %param.8, bf16[128,2048]{1,0:T(8,128)(2,1)S(1)} %copy-done.3, f32[2048]{0:T(1024)S(1)} %convert_element_type.61, f32[128]{0:T(128)S(1)} %add_rsqrt_fusion), kind=kOutput, calls=%fused_computation.11 | convolution fusion | flops 4296015872 | bytes 38281728 | tf_op jit(solution)/shard_map/dot_general | solution.py:46
  67.9 2.5 copy.16
  70.4 5.3 %all-to-all-start.1 = ((f32[4,128,2048]{2,1,0:T(8,128)}), f32[4,128,2048]{2,1,0:T(8,128)}, u32[]{:S(2)}, u32[]{:S(2)}) async-start(f32[4,128,2048]{2,1,0:T(8,128)} %bitcast.39), calls=%async_computation.2 | async-start | bytes 8388608 | tf_op jit(solution)/shard_map/all_to_all | solution.py:48
  75.7 0.0 all-gather.3.cloned.1.call-start
  75.7 0.0 copy-done.5
  75.7 0.1 broadcast_in_dim.2
  75.8 0.1 div.35
  75.9 46.4 %all-to-all-done.1 = f32[4,128,2048]{2,1,0:T(8,128)} async-done(((f32[4,128,2048]{2,1,0:T(8,128)}), f32[4,128,2048]{2,1,0:T(8,128)}, u32[]{:S(2)}, u32[]{:S(2)}) %all-to-all-start.1) | async-done | bytes 4194336 | tf_op jit(solution)/shard_map/all_to_all | solution.py:48
  122.3 2.7 reduce_sum.65
  125.1 0.1 reduce_max.19
  125.2 0.3 exponential_reduce_fusion
  125.5 70.3 %reduce-scatter.2.cloned.1.call-done = f32[128,2048]{1,0:T(8,128)} async-done(((f32[1024,2048]{1,0:T(8,128)}), f32[128,2048]{1,0:T(8,128)}) %reduce-scatter.2.cloned.1.call-update) | async-done | bytes 1048592 | tf_op jit(solution)/shard_map/reduce_scatter | solution.py:37
  195.8 1.4 reduce_max.18
  197.2 1.5 exponential_reduce_fusion.1
  198.7 2.6 multiply_reduce_fusion
  201.3 0.0 all-gather.3.cloned.1.call-update
  201.3 0.1 div.36
  201.4 5.0 %all-gather = f32[4,1,128]{2,1,0:T(1,128)S(1)} all-gather(f32[1,1,128]{2,1,0:T(1,128)S(1)} %fusion.12), channel_id=1, replica_groups=mesh['group'=2,'dp'=8,'mp'=2] {'group','mp'}, dimensions={0}, use_global_device_ids=true | all-gather | bytes 2560 | tf_op jit(solution)/shard_map/all_gather | solution.py:81
  206.4 67.4 %all-gather.3.cloned.1.call-done = bf16[1024,2048]{1,0:T(8,128)(2,1)} async-done(((bf16[128,2048]{1,0:T(8,128)(2,1)}), bf16[1024,2048]{1,0:T(8,128)(2,1)}) %all-gather.3.cloned.1.call-update) | async-done | bytes 4194320 | tf_op jit(solution)/shard_map/all_gather | solution.py:84
  273.9 5.7 %convolution_convert_fusion = bf16[1024,512]{1,0:T(8,128)(2,1)} fusion(bf16[1024,2048]{1,0:T(8,128)(2,1)} %all-gather.3.cloned.1.call-done, bf16[512,2048]{1,0:T(8,128)(2,1)S(1)} %copy-done), kind=kOutput, calls=%fused_computation.1 | convolution fusion | flops 2148007936 | bytes 7340032 | tf_op jit(solution)/shard_map/dot_general | solution.py:86
  279.5 4.7 %all-to-all-start.2 = ((bf16[4,256,512]{2,1,0:T(8,128)(2,1)}), bf16[4,256,512]{2,1,0:T(8,128)(2,1)}, u32[]{:S(2)}, u32[]{:S(2)}) async-start(bf16[4,256,512]{2,1,0:T(8,128)(2,1)} %bitcast.44), calls=%async_computation.3 | async-start | bytes 2097152 | tf_op jit(solution)/shard_map/all_to_all | solution.py:91
  284.3 0.0 copy-done.2
  284.3 6.6 %fusion.14 = f32[512,2048]{1,0:T(8,128)} fusion(bf16[512,1024]{0,1:T(8,128)(2,1)S(1)} %bitcast.41, bf16[1024,2048]{1,0:T(8,128)(2,1)} %all-gather.3.cloned.1.call-done), kind=kOutput, calls=%fused_computation.31 | convolution fusion | flops 2147483648 | bytes 9437184 | tf_op jit(solution)/shard_map/dot_general | solution.py:92
  290.8 6.3 %all-to-all-done.2 = bf16[4,256,512]{2,1,0:T(8,128)(2,1)} async-done(((bf16[4,256,512]{2,1,0:T(8,128)(2,1)}), bf16[4,256,512]{2,1,0:T(8,128)(2,1)}, u32[]{:S(2)}, u32[]{:S(2)}) %all-to-all-start.2) | async-done | bytes 1048608 | tf_op jit(solution)/shard_map/all_to_all | solution.py:91
  297.2 1.5 reduce_sum.69
  298.7 2.7 collective-permute-start.1
  301.4 3.0 collective-permute-start
  304.5 8.2 %collective-permute-done.1 = bf16[128,512]{1,0:T(8,128)(2,1)S(1)} collective-permute-done((bf16[128,512]{1,0:T(8,128)(2,1)S(1)}, bf16[128,512]{1,0:T(8,128)(2,1)S(1)}, u32[]{:S(2)}, u32[]{:S(2)}) %collective-permute-start.1) | collective-permute-done | bytes 131104 | tf_op jit(solution)/shard_map/ppermute | solution.py:113
  312.6 1.5 collective-permute-done
  314.1 0.1 fusion.10
  314.2 0.8 maximum_convert_fusion
  315.0 0.6 copy.18
  (9 shorter events, 0.1 us)
Async XLA Ops:
  7.2 34.8 %copy-start = (bf16[512,2048]{1,0:T(8,128)(2,1)S(1)}, bf16[512,2048]{1,0:T(8,128)(2,1)}, u32[]{:S(2)}) copy-start(bf16[512,2048]{1,0:T(8,128)(2,1)} %param.10) | copy-start | bytes 6291460
  7.2 188.6 %reduce-scatter.2.cloned.1.call-start = ((), (), s32[]{:S(2)}) async-start(), calls=%async_computation.4 | async-start | bytes 9437184 | tf_op jit(solution)/shard_map/reduce_scatter | solution.py:37
  42.0 5.6 %copy-start.1 = (bf16[8,128,512]{2,1,0:T(8,128)(2,1)}, bf16[8,128,512]{2,1,0:T(8,128)(2,1)S(1)}, u32[]{:S(2)}) copy-start(bf16[8,128,512]{2,1,0:T(8,128)(2,1)S(1)} %copy.12) | copy-start | bytes 3145732
  47.6 0.7 copy-start.4
  47.6 1.1 copy-start.3
  70.4 5.3 %copy-start.5 = (s32[2]{0:T(128)S(1)}, s32[2]{0:T(128)}, u32[]{:S(2)}) copy-start(s32[2]{0:T(128)} %param.11) | copy-start | bytes 28
  70.4 51.9 %all-to-all-start.1 = ((f32[4,128,2048]{2,1,0:T(8,128)}), f32[4,128,2048]{2,1,0:T(8,128)}, u32[]{:S(2)}, u32[]{:S(2)}) async-start(f32[4,128,2048]{2,1,0:T(8,128)} %bitcast.39), calls=%async_computation.2 | async-start | bytes 8388608 | tf_op jit(solution)/shard_map/all_to_all | solution.py:48
  75.7 198.1 %all-gather.3.cloned.1.call-start = ((), (), s32[]{:S(2)}) async-start(), calls=%async_computation.5 | async-start | bytes 4718592 | tf_op jit(solution)/shard_map/all_gather | solution.py:84
  273.9 10.4 %copy-start.2 = (bf16[8,128,512]{2,1,0:T(8,128)(2,1)S(1)}, bf16[8,128,512]{2,1,0:T(8,128)(2,1)}, u32[]{:S(2)}) copy-start(bf16[8,128,512]{2,1,0:T(8,128)(2,1)} %copy-done.1) | copy-start | bytes 3145732
  279.5 17.7 %all-to-all-start.2 = ((bf16[4,256,512]{2,1,0:T(8,128)(2,1)}), bf16[4,256,512]{2,1,0:T(8,128)(2,1)}, u32[]{:S(2)}, u32[]{:S(2)}) async-start(bf16[4,256,512]{2,1,0:T(8,128)(2,1)} %bitcast.44), calls=%async_computation.3 | async-start | bytes 2097152 | tf_op jit(solution)/shard_map/all_to_all | solution.py:91
  298.7 14.0 %collective-permute-start.1 = (bf16[128,512]{1,0:T(8,128)(2,1)S(1)}, bf16[128,512]{1,0:T(8,128)(2,1)S(1)}, u32[]{:S(2)}, u32[]{:S(2)}) collective-permute-start(bf16[128,512]{1,0:T(8,128)(2,1)S(1)} %get-tuple-element.21), channel_id=1, source_target_pairs={{0,2},{1,6},{16,10},{17,14},{2,0},{3,4},{18,8},{19,12},{4,3},{5,7}... | collective-permute-start | bytes 393224 | tf_op jit(solution)/shard_map/ppermute | solution.py:113
  301.4 12.7 %collective-permute-start = (bf16[128,512]{1,0:T(8,128)(2,1)S(1)}, bf16[128,512]{1,0:T(8,128)(2,1)S(1)}, u32[]{:S(2)}, u32[]{:S(2)}) collective-permute-start(bf16[128,512]{1,0:T(8,128)(2,1)S(1)} %get-tuple-element.22), channel_id=1, source_target_pairs={{0,0},{1,4},{16,8},{17,12},{2,2},{3,6},{18,10},{19,14},{4,1},{5,5}... | collective-permute-start | bytes 393224 | tf_op jit(solution)/shard_map/ppermute | solution.py:113
Sparse Core Ops, SparseCore 0:
  47.7 148.0 reduce-scatter.1
  201.4 72.3 all-gather.2
